TPU v7x, 32 devices: a whole 2x2x4 slice. The times are simulated.
32 devices in a mesh: seq: 8 (over z, x), dp: 4 (over y, core).
Axes of the slice: x: 2, y: 2, z: 4, core: 2. Of those that a mesh axis runs over, the one named last changes fastest.
Arguments:
- linear_queries: bfloat16 [4, 1024, 2048], P('dp', 'seq'), may hold values from -6 to 6
- linear_keys: bfloat16 [4, 1024, 2048], P('dp', 'seq'), may hold values from -6 to 6
- window_queries: bfloat16 [4, 1024, 2048], P('dp', 'seq'), may hold values from -41 to 41
- window_keys: bfloat16 [4, 1024, 2048], P('dp', 'seq'), may hold values from -12 to 12
- values: bfloat16 [4, 1024, 2048], P('dp', 'seq'), may hold values from -8 to 8
- cotangent: bfloat16 [4, 1024, 2048], P('dp', 'seq'), may hold values from -10 to 10
- feature_map: bfloat16 [16, 128, 128], replicated, may hold values from -0.5 to 0.5
Outputs:
- attended: bfloat16 [4, 1024, 2048], P('dp', 'seq')
- dlinear_queries: bfloat16 [4, 1024, 2048], P('dp', 'seq')
- dlinear_keys: bfloat16 [4, 1024, 2048], P('dp', 'seq')
- dwindow_queries: bfloat16 [4, 1024, 2048], P('dp', 'seq')
- dwindow_keys: bfloat16 [4, 1024, 2048], P('dp', 'seq')
- dvalues: bfloat16 [4, 1024, 2048], P('dp', 'seq')
- dfeature_map: float32 [16, 128, 128], replicated
All inputs are finite; a program needn't handle non-finite values.
Results may differ from a plain program's by a relative error of at most 0.009.
Values may be sent and summed in bfloat16 or wider, within the bound.
No kernel may reach another device: no remote copies, remote signals or barrier semaphores. Data moves between devices by JAX's collectives and lax.ppermute only.
A program may use at most 192 MiB of HBM per device.

v0:
```python
import jax
import jax.numpy as jnp
from jax import lax
from jax.sharding import PartitionSpec as P

HEADS = 16
HD = 128
WINDOW = 64


def entering(shard, axis, join, neutral, backward):
    count = lax.axis_size(axis)
    place = lax.axis_index(axis)
    ahead = count - 1 - place if backward else place
    gathered = lax.all_gather(shard.astype(jnp.bfloat16), axis)
    state = jnp.zeros_like(shard) + jnp.asarray(neutral, shard.dtype)

    def one(turn, state):
        source = count - 1 - turn if backward else turn
        return join(state, lax.dynamic_index_in_dim(gathered, source, 0, False).astype(shard.dtype))

    return lax.fori_loop(0, ahead, one, state)


def passed_along(block, axis, distance):
    devices = range(lax.axis_size(axis))
    route = [(i - distance, i) for i in devices if i - distance in devices]
    return lax.ppermute(block, axis, route)


def plain(form, left, right):
    return jnp.einsum(form, left, right, preferred_element_type=jnp.float32)


def exact(form, left, right):
    return jnp.einsum(
        form, left.astype(jnp.float32), right.astype(jnp.float32), precision=lax.Precision.HIGHEST
    )


def feature(inputs, feature_map):
    before = plain("htd,hde->hte", inputs, feature_map)
    mapped = jnp.where(before > 0, before + 1.0, jnp.exp(jnp.minimum(before, 0.0)))
    return (before, mapped.astype(jnp.bfloat16))


def slope(before):
    return jnp.where(before > 0, 1.0, jnp.exp(jnp.minimum(before, 0.0)))


def split_heads(matrix):
    return matrix.reshape(matrix.shape[0], HEADS, HD).transpose(1, 0, 2)


def join_heads(tensor):
    return tensor.transpose(1, 0, 2).reshape(tensor.shape[1], HEADS * HD)


def exclusive(terms, reverse):
    zero = jnp.zeros_like(terms[:1])
    if reverse:
        totals = jnp.flip(jnp.cumsum(jnp.flip(terms, 0), axis=0), 0)
        return jnp.concatenate([totals[1:], zero], axis=0)
    totals = jnp.cumsum(terms, axis=0)
    return jnp.concatenate([zero, totals[:-1]], axis=0)


def band_mask():
    rows = lax.broadcasted_iota(jnp.int32, (WINDOW, 2 * WINDOW), 0)
    cols = lax.broadcasted_iota(jnp.int32, (WINDOW, 2 * WINDOW), 1)
    offset = cols - rows
    return (offset >= 1) & (offset <= WINDOW)


def window_mask(blocks, start):
    cols = lax.broadcasted_iota(jnp.int32, (blocks, WINDOW, 2 * WINDOW), 2)
    block = lax.broadcasted_iota(jnp.int32, (blocks, WINDOW, 2 * WINDOW), 0)
    keypos = start + block * WINDOW + cols - WINDOW
    return band_mask()[None] & (keypos >= 0)


def causal_mask():
    rows = lax.broadcasted_iota(jnp.int32, (WINDOW, WINDOW), 0)
    cols = lax.broadcasted_iota(jnp.int32, (WINDOW, WINDOW), 1)
    return rows >= cols


def pairs(rim, inputs):
    blocks = inputs.shape[1] // WINDOW
    early = jnp.concatenate([rim, inputs[:, : inputs.shape[1] - WINDOW]], axis=1).reshape(
        HEADS, blocks, WINDOW, HD
    )
    late = inputs.reshape(HEADS, blocks, WINDOW, HD)
    return jnp.concatenate([early, late], axis=2)


def softmax_rows(score, mask):
    top = jnp.max(jnp.where(mask, score, -jnp.inf), axis=-1, keepdims=True)
    expo = jnp.exp(jnp.where(mask, score - top, -jnp.inf))
    return expo / jnp.sum(expo, axis=-1, keepdims=True)


def fold_pairs(pair, rim):
    after = jnp.concatenate([pair[:, 1:, :WINDOW], rim[:, None]], axis=1)
    return pair[:, :, WINDOW:] + after


def add_up(earlier, later):
    return earlier + later


def carry_states(totals, reverse):
    if reverse:
        return entering(totals, "seq", add_up, jnp.zeros_like(totals), True)
    return entering(totals, "seq", add_up, jnp.zeros_like(totals), False)


def on_device(
    linear_queries, linear_keys, window_queries, window_keys, values, cotangent, feature_map
):
    tokens = linear_queries.shape[1]
    blocks = tokens // WINDOW
    block_shape = (HEADS, blocks, WINDOW, HD)
    length = tokens * lax.axis_size("seq")
    lin_scale = 1.0 / (HD * length)
    inverse_root = HD ** (-0.5)
    win_heads = split_heads(window_queries[0])
    wkey_heads = split_heads(window_keys[0])
    value_heads = split_heads(values[0])
    grad_full = split_heads(cotangent[0])
    key_rim, value_rim = passed_along(
        (wkey_heads[:, tokens - WINDOW :], value_heads[:, tokens - WINDOW :]), "seq", 1
    )
    query_heads = split_heads(linear_queries[0])
    key_heads = split_heads(linear_keys[0])
    pre_query, feat_query = feature(query_heads, feature_map)
    pre_key, feat_key = feature(key_heads, feature_map)
    query_blocks = feat_query.reshape(block_shape)
    key_blocks = feat_key.reshape(block_shape)
    value_blocks = value_heads.reshape(block_shape)
    causal = causal_mask()
    lin_scores = jnp.where(causal, plain("hncf,hnsf->hncs", query_blocks, key_blocks), 0.0)
    block_states = plain("hnsf,hnsd->nhfd", key_blocks, value_blocks)
    state_in = carry_states(jnp.sum(block_states, axis=0), False)[None] + exclusive(
        block_states, False
    )
    lin = (
        exact("hncs,hnsd->hncd", lin_scores, value_blocks)
        + exact("hncf,nhfd->hncd", query_blocks, state_in)
    ) * lin_scale
    win_queries = win_heads.reshape(block_shape)
    key_pairs = pairs(key_rim, wkey_heads)
    value_pairs = pairs(value_rim, value_heads)
    mask = window_mask(blocks, lax.axis_index("seq") * tokens)
    prob = softmax_rows(plain("hncd,hnsd->hncs", win_queries, key_pairs) * inverse_root, mask[None])
    prob_b = prob.astype(jnp.bfloat16)
    win = plain("hncs,hnsd->hncd", prob_b, value_pairs)
    attended = join_heads((lin + win).astype(jnp.bfloat16).reshape(HEADS, tokens, HD))
    grad_heads = grad_full.reshape(block_shape)
    grad_lin = grad_heads.astype(jnp.float32) * lin_scale
    mixed = jnp.where(causal, plain("hncd,hnsd->hncs", grad_heads, value_blocks), 0.0) * lin_scale
    dfeat_query = exact("hncs,hnsf->hncf", mixed, key_blocks) + exact(
        "hncd,nhfd->hncf", grad_lin, state_in
    )
    grad_states = plain("hncf,hncd->nhfd", query_blocks, grad_heads) * lin_scale
    state_after = carry_states(jnp.sum(grad_states, axis=0), True)[None] + exclusive(
        grad_states, True
    )
    dfeat_key = exact("hncs,hncf->hnsf", mixed, query_blocks) + exact(
        "nhfd,hnsd->hnsf", state_after, value_blocks
    )
    dvalue_lin = exact("hncs,hncd->hnsd", lin_scores, grad_lin) + exact(
        "hnsf,nhfd->hnsd", key_blocks, state_after
    )
    dpre_query = (dfeat_query.reshape(HEADS, tokens, HD) * slope(pre_query)).astype(jnp.bfloat16)
    dpre_key = (dfeat_key.reshape(HEADS, tokens, HD) * slope(pre_key)).astype(jnp.bfloat16)
    dlin_queries = join_heads(plain("htf,hdf->htd", dpre_query, feature_map).astype(jnp.bfloat16))
    dlin_keys = join_heads(plain("htf,hdf->htd", dpre_key, feature_map).astype(jnp.bfloat16))
    map_terms = plain("htd,hte->hde", query_heads, dpre_query) + plain(
        "htd,hte->hde", key_heads, dpre_key
    )
    dprob = plain("hncd,hnsd->hncs", grad_heads, value_pairs)
    delta = jnp.sum(prob * dprob, axis=-1, keepdims=True)
    dscore = (prob * (dprob - delta) * inverse_root).astype(jnp.bfloat16)
    dwin_queries = join_heads(
        plain("hncs,hnsd->hncd", dscore, key_pairs).reshape(HEADS, tokens, HD).astype(jnp.bfloat16)
    )
    key_pair_grads = plain("hncs,hncd->hnsd", dscore, win_queries)
    value_pair_grads = plain("hncs,hncd->hnsd", prob_b, grad_heads)
    rim_keys, rim_values = (
        passed_along(key_pair_grads[:, 0, :WINDOW].astype(jnp.bfloat16), "seq", -1).astype(
            jnp.float32
        ),
        passed_along(value_pair_grads[:, 0, :WINDOW].astype(jnp.bfloat16), "seq", -1).astype(
            jnp.float32
        ),
    )
    dkey_win = fold_pairs(key_pair_grads, rim_keys)
    dvalue_win = fold_pairs(value_pair_grads, rim_values)
    dwin_keys = join_heads(dkey_win.reshape(HEADS, tokens, HD).astype(jnp.bfloat16))
    dvalue_all = join_heads(
        (dvalue_lin + dvalue_win).reshape(HEADS, tokens, HD).astype(jnp.bfloat16)
    )
    total_tokens = length * lax.axis_size("dp") * linear_queries.shape[0]
    map_grad = lax.psum(map_terms, ("seq", "dp")) * total_tokens ** (-0.5)
    return (
        attended[None],
        dlin_queries[None],
        dlin_keys[None],
        dwin_queries[None],
        dwin_keys[None],
        dvalue_all[None],
        map_grad,
    )


def solution(mesh):
    return jax.shard_map(
        on_device,
        mesh=mesh,
        in_specs=(
            P("dp", "seq", None),
            P("dp", "seq", None),
            P("dp", "seq", None),
            P("dp", "seq", None),
            P("dp", "seq", None),
            P("dp", "seq", None),
            P(),
        ),
        out_specs=(
            P("dp", "seq", None),
            P("dp", "seq", None),
            P("dp", "seq", None),
            P("dp", "seq", None),
            P("dp", "seq", None),
            P("dp", "seq", None),
            P(),
        ),
        check_vma=False,
    )
```

profile of v0, /device:TPU:0, one launch (start us, length us, event | category | flops | bytes accessed | tf_op | source)
XLA Modules:
  0.0 374.6 jit_solution(10899480268621206970)
XLA Ops:
  8.4 1.3 copy.140
  10.4 2.8 multiply_reduce_fusion
  13.3 3.2 reverse.4
  17.7 1.3 fusion.57
  19.0 1.4 fusion.34
  20.4 69.1 %all-gather.7.cloned.1.call-done = bf16[128,128,128]{2,1,0:T(8,128)(2,1)} async-done(((bf16[16,128,128]{2,1,0:T(8,128)(2,1)}), bf16[128,128,128]{2,1,0:T(8,128)(2,1)}) %all-gather.7.cloned.1.call-update) | async-done | bytes 4194320 | tf_op jit(solution)/shard_map/all_gather | solution.py:15
  89.6 9.2 %while.23 = (s32[]{:T(128)}, f32[16,128,128]{2,1,0:T(8,128)S(1)}, s32[]{:T(128)}, bf16[8,16,128,128]{3,2,1,0:T(8,128)(2,1)}, s32[]{:T(128)}, /*index=5*/s32[]{:T(128)}, s32[]{:T(128)}, s32[]{:T(128)}) while((s32[]{:T(128)}, f32[16,128,128]{2,1,0:T(8,128)S(1)}, s32[]{:T(128)}, bf16[8,16,128,128]{3,2,1,0:T(8,128)(2,1)}, s32[]{:T(128)}, ...), condition=%wide.region_8.9_spmd, body=%wide.region_7.8_spmd.sunk | while | flops 524294 | bytes 2621575 | solution.py:22
  89.6 1.3 convert_add_fusion.5
  90.9 1.3 convert_add_fusion.5
  92.2 1.3 convert_add_fusion.5
  93.5 1.3 convert_add_fusion.5
  94.8 1.3 convert_add_fusion.5
  98.8 2.0 select_add_fusion
  100.8 2.3 fusion.14
  105.3 2.8 fusion.112
  111.0 2.0 collective-permute-start
  113.7 2.2 collective-permute-start.1
  117.4 7.1 %collective-permute-done = bf16[16,64,128]{2,1,0:T(8,128)(2,1)} collective-permute-done((bf16[16,64,128]{2,1,0:T(8,128)(2,1)}, bf16[16,64,128]{2,1,0:T(8,128)(2,1)}, u32[]{:S(2)}, u32[]{:S(2)}) %collective-permute-start) | collective-permute-done | bytes 262176 | tf_op jit(solution)/shard_map/ppermute | solution.py:28
  125.6 2.9 collective-permute-done.1
  129.5 1.8 convolution_bitcast_fusion
  133.1 1.4 fusion.113
  134.5 15.4 %fusion.51 = f32[16,2,128,128]{3,2,1,0:T(8,128)} fusion(bf16[16,2,64,128]{3,2,1,0:T(8,128)(2,1)} %bitcast.171, f32[16,2,64,128]{3,2,1,0:T(8,128)} %convolution_bitcast_fusion, f32[16,2,64,128]{3,2,1,0:T(8,128)} %get-tuple-element.151, f32[16,2,64]{2,1,0:T(2,128)S(1)} %get-tuple-element.150), kind=kOutput, calls=%fused_computation.71 | convolution fusion | flops 68946048 | bytes 4726784 | tf_op jit(solution)/shard_map/hncs,hncd->hnsd/dot_general | solution.py:32
  149.9 1.8 fusion.81
  151.7 1.5 collective-permute-start.2
  153.2 7.1 %fusion.83 = f32[16,2,128,128]{3,2,1,0:T(8,128)} fusion(bf16[16,2,64,128]{3,2,1,0:T(8,128)(2,1)S(1)} %bitcast.154, f32[16,2,64]{2,1,0:T(2,128)S(1)} %get-tuple-element.150, f32[16,2,64,128]{3,2,1,0:T(8,128)} %copy-done.20, pred[2,64,128]{2,1,0:T(8,128)(4,1)S(1)} %fusion.86), kind=kOutput, calls=%fused_computation.111 | convolution fusion | flops 68421760 | bytes 3694592 | tf_op jit(solution)/shard_map/hncs,hncd->hnsd/dot_general | solution.py:32
  160.2 1.8 fusion.82
  162.0 14.3 %convolution_convert_fusion.2 = bf16[16,2,64,128]{3,2,1,0:T(8,128)(2,1)} fusion(f32[16,2,64,128]{3,2,1,0:T(8,128)} %convolution_bitcast_fusion, bf16[16,2,64,128]{3,2,1,0:T(8,128)(2,1)} %bitcast.160, bf16[16,2,64,128]{3,2,1,0:T(8,128)(2,1)} %bitcast.173, f32[16,2,64,128]{3,2,1,0:T(8,128)} %get-tuple-element.151, f32[16,2,64]{2,1,0:T(2,128)S(1)} %get-tuple-element.150), kind=kOutput, calls=%fused_computation.43 | convolution fusion | flops 71305344 | bytes 3678208 | tf_op jit(solution)/shard_map/hncs,hnsd->hncd/dot_general | solution.py:32
  176.4 1.9 slice.58
  179.6 2.2 copy.114
  181.7 2.1 broadcast_in_dim_reshape.21
  185.9 1.4 fusion.49
  188.1 2.0 copy.118
  190.2 2.0 copy.127
  192.3 1.8 fusion.114
  198.1 1.9 fusion.48
  201.2 2.1 broadcast_in_dim_reshape.23
  203.3 1.3 convolution_convert_fusion
  204.6 2.0 copy.126
  206.6 2.8 fusion.115
  209.8 5.7 %fusion.17 = f32[16,2,64,128]{3,2,1,0:T(8,128)S(1)} fusion(f32[16,2,64,128]{3,2,1,0:T(8,128)} %fusion.115, bf16[16,2,64,128]{3,2,1,0:T(8,128)(2,1)S(1)} %bitcast.156, f32[1,16,128,128]{3,2,1,0:T(8,128)} %slice.49, f32[16,128,128]{2,1,0:T(8,128)S(1)} %get-tuple-element.86), kind=kOutput, calls=%fused_computation.20 | convolution fusion | flops 403963904 | bytes 4718592 | tf_op jit(solution)/shard_map/hncd,nhfd->hncf/dot_general | solution.py:36
  216.9 1.3 convolution_convert_fusion.1
  218.2 2.1 fusion.10
  220.4 1.4 fusion.31
  222.8 2.9 fusion.33
  225.7 5.6 %fusion.35 = bf16[16,2,64,128]{3,2,1,0:T(8,128)(2,1)S(1)} fusion(f32[16,2,64,128]{3,2,1,0:T(8,128)} %fusion.33, bf16[16,2,64,128]{3,2,1,0:T(8,128)(2,1)S(1)} %bitcast.143, bf16[16,2,64,128]{3,2,1,0:T(8,128)(2,1)S(1)} %bitcast.169, f32[16,2,64]{2,1,0:T(2,128)S(1)} %get-tuple-element.150, f32[16,2,64,128]{3,2,1,0:T(8,128)} %copy-done.20, ...), kind=kOutput, calls=%fused_computation.40 | convolution fusion | flops 71043200 | bytes 3694592 | tf_op jit(solution)/shard_map/hncs,hnsd->hncd/dot_general | solution.py:32
  232.7 132.8 %all-reduce.3.cloned.1.call-done = f32[16,128,128]{1,2,0:T(8,128)} async-done(((f32[16,128,128]{1,2,0:T(8,128)}), f32[16,128,128]{1,2,0:T(8,128)}) %all-reduce.3.cloned.1.call-update) | async-done | bytes 1048592 | tf_op jit(solution)/shard_map/psum | solution.py:205
  365.5 1.3 broadcast_multiply_fusion
  366.8 1.3 copy.128
  (114 shorter events, 30.3 us)
Async XLA Ops:
  7.2 2.6 copy-start
  7.2 82.3 %all-gather.7.cloned.1.call-start = ((), (), s32[]{:S(2)}) async-start(), calls=%async_computation.2 | async-start | bytes 4718592 | tf_op jit(solution)/shard_map/all_gather | solution.py:15
  8.4 1.7 copy-start.15
  10.1 3.1 copy-start.7
  13.2 196.2 %all-gather.5.cloned.1.call-start = ((), (), s32[]{:S(2)}) async-start(), calls=%async_computation.1 | async-start | bytes 4718592 | tf_op jit(solution)/shard_map/all_gather | solution.py:15
  13.3 3.2 copy-start.29
  16.5 1.1 copy-start.30
  16.6 0.8 copy-start.11
  17.7 2.7 copy-start.17
  89.6 9.2 %copy-start.31 = (pred[2]{0:T(512)(128)(4,1)S(1)}, pred[2]{0:T(512)(128)(4,1)}, u32[]{:S(2)}) copy-start(pred[2]{0:T(512)(128)(4,1)} %constant.73.clone.1) | copy-start | bytes 10
  100.8 3.4 copy-start.1
  100.8 2.3 copy-start.5
  103.1 1.2 copy-start.19
  104.2 1.1 copy-start.12
  104.7 98.5 %copy-start.9 = (bf16[16,128,128]{2,1,0:T(8,128)(2,1)}, bf16[16,128,128]{2,1,0:T(8,128)(2,1)S(1)}, u32[]{:S(2)}) copy-start(bf16[16,128,128]{2,1,0:T(8,128)(2,1)S(1)} %get-tuple-element.132) | copy-start | bytes 1572868
  108.0 257.4 %all-reduce.3.cloned.1.call-start = ((), (), s32[]{:S(2)}) async-start(), calls=%async_computation | async-start | bytes 2097152 | tf_op jit(solution)/shard_map/psum | solution.py:205
  109.4 0.8 copy-start.13
  111.0 13.5 %collective-permute-start = (bf16[16,64,128]{2,1,0:T(8,128)(2,1)}, bf16[16,64,128]{2,1,0:T(8,128)(2,1)}, u32[]{:S(2)}, u32[]{:S(2)}) collective-permute-start(bf16[16,64,128]{2,1,0:T(8,128)(2,1)} %get-tuple-element.134), channel_id=1, source_target_pairs={{0,4},{4,8},{8,12},{12,16},{16,20},{20,24},{24,28},{1,5},{5,9},{9,... | collective-permute-start | bytes 786440 | tf_op jit(solution)/shard_map/ppermute | solution.py:28
  113.7 14.8 %collective-permute-start.1 = (bf16[16,64,128]{2,1,0:T(8,128)(2,1)}, bf16[16,64,128]{2,1,0:T(8,128)(2,1)}, u32[]{:S(2)}, u32[]{:S(2)}) collective-permute-start(bf16[16,64,128]{2,1,0:T(8,128)(2,1)} %get-tuple-element.138), channel_id=1, source_target_pairs={{0,4},{4,8},{8,12},{12,16},{16,20},{20,24},{24,28},{1,5},{5,9},{9,... | collective-permute-start | bytes 786440 | tf_op jit(solution)/shard_map/ppermute | solution.py:28
  116.0 8.6 %copy-start.28 = (bf16[16,64,128]{2,1,0:T(8,128)(2,1)S(1)}, bf16[16,64,128]{2,1,0:T(8,128)(2,1)}, u32[]{:S(2)}) copy-start(bf16[16,64,128]{2,1,0:T(8,128)(2,1)} %get-tuple-element.135) | copy-start | bytes 786436
  117.3 14.0 %copy-start.24 = (bf16[16,128,128]{2,1,0:T(8,128)(2,1)}, bf16[16,128,128]{2,1,0:T(8,128)(2,1)S(1)}, u32[]{:S(2)}) copy-start(bf16[16,128,128]{2,1,0:T(8,128)(2,1)S(1)} %copy.106) | copy-start | bytes 1572868
  125.5 6.6 %copy-start.25 = (bf16[16,128,128]{2,1,0:T(8,128)(2,1)}, bf16[16,128,128]{2,1,0:T(8,128)(2,1)S(1)}, u32[]{:S(2)}) copy-start(bf16[16,128,128]{2,1,0:T(8,128)(2,1)S(1)} %pad_maximum_fusion.6) | copy-start | bytes 1572868
  125.6 5.7 %copy-start.14 = (bf16[128,16,128]{2,0,1:T(8,128)(2,1)S(1)}, bf16[128,16,128]{2,0,1:T(8,128)(2,1)}, u32[]{:S(2)}) copy-start(bf16[128,16,128]{2,0,1:T(8,128)(2,1)} %copy-done.13) | copy-start | bytes 1572868
  129.5 1.8 copy-start.21
  132.1 1.0 copy-start.20
  151.7 33.2 %collective-permute-start.2 = (bf16[16,64,128]{2,1,0:T(8,128)(2,1)}, bf16[16,64,128]{2,1,0:T(8,128)(2,1)}, u32[]{:S(2)}, u32[]{:S(2)}) collective-permute-start(bf16[16,64,128]{2,1,0:T(8,128)(2,1)} %fusion.81), channel_id=1, source_target_pairs={{4,0},{8,4},{12,8},{16,12},{20,16},{24,20},{28,24},{5,1},{9,5},{13... | collective-permute-start | bytes 786440 | tf_op jit(solution)/shard_map/ppermute | solution.py:28
  178.3 13.9 %collective-permute-start.3 = (bf16[16,64,128]{2,1,0:T(8,128)(2,1)}, bf16[16,64,128]{2,1,0:T(8,128)(2,1)S(1)}, u32[]{:S(2)}, u32[]{:S(2)}) collective-permute-start(bf16[16,64,128]{2,1,0:T(8,128)(2,1)} %fusion.82), channel_id=1, source_target_pairs={{4,0},{8,4},{12,8},{16,12},{20,16},{24,20},{28,24},{5,1},{9,5},{13... | collective-permute-start | bytes 786440 | tf_op jit(solution)/shard_map/ppermute | solution.py:28
  194.0 2.0 copy-start.2
  196.0 4.1 %copy-start.3 = (f32[16,2,64,64]{3,2,1,0:T(8,128)}, f32[16,2,64,64]{3,2,1,0:T(8,128)S(1)}, u32[]{:S(2)}) copy-start(f32[16,2,64,64]{3,2,1,0:T(8,128)S(1)} %convolution_select_fusion.1) | copy-start | bytes 1572868
  196.0 1.4 copy-start.23
  196.0 2.1 copy-start.27
  209.8 5.7 %copy-start.8 = (f32[16,128,128]{2,1,0:T(8,128)S(1)}, f32[16,128,128]{2,1,0:T(8,128)}, u32[]{:S(2)}) copy-start(f32[16,128,128]{2,1,0:T(8,128)} %copy-done.7) | copy-start | bytes 3145732
  215.5 1.0 copy-start.16
  216.6 1.6 copy-start.6
  218.2 2.1 copy-start.10
  218.2 2.1 copy-start.18
  220.4 1.4 copy-start.26
  220.4 2.4 copy-start.4
  222.8 2.9 copy-start.22
Sparse Core Ops, SparseCore 0:
  13.3 76.0 all-gather.6
  108.2 82.5 all-gather.4
  221.9 143.5 all-reduce.2
where the time goes:
time: 376 us; the launch traced here: 375 us
  waiting for transfers between devices  212 us (56%)
  matrix products  78.2 us (21%)
  local copies, waits for them, and re-layouts  41.8 us (11%)
  other arithmetic  20.9 us (6%)
  between operations  14.3 us (4%)
  starting transfers between devices  7.03 us (2%)
    psum x1, waiting for transfers between devices, on_device(): map_grad = lax.psum(map_terms, ('seq', 'dp')) * total_tokens ** (-0.5)  133 us
    all_gather x2, waiting for transfers between devices, entering(): gathered = lax.all_gather(shard.astype(jnp.bfloat16), axis)  69.1 us
    dot_general x16, matrix products, plain(): return jnp.einsum(form, left, right, preferred_element_type=jnp.float32)  58.2 us
    dot_general x8, matrix products, exact(): jnp.einsum(form, left.astype(jnp.float32), right.astype(jnp.float32), pre...  20 us
    unnamed x75, local copies, waits for them, and re-layouts  18 us
    ppermute x4, waiting for transfers between devices, passed_along(): return lax.ppermute(block, axis, route)  10.1 us
    add x7, other arithmetic, add_up(): return earlier + later  8.98 us
  transfers between devices with their start and end apart: 7, of which 4 were waited for; matrix products, arithmetic and copies ran while one was open for 26% of the time, Pallas kernels for 0%

commit v1 on v0

--- a/solution.py
+++ b/solution.py
@@ -202,7 +202,9 @@
         (dvalue_lin + dvalue_win).reshape(HEADS, tokens, HD).astype(jnp.bfloat16)
     )
     total_tokens = length * lax.axis_size("dp") * linear_queries.shape[0]
-    map_grad = lax.psum(map_terms, ("seq", "dp")) * total_tokens ** (-0.5)
+    map_grad = lax.psum(lax.psum(map_terms, axis_name="dp"), axis_name="seq") * total_tokens ** (
+        -0.5
+    )
     return (
         attended[None],
         dlin_queries[None],

time: 376 us -> 345 us (0.918)
  waiting for transfers between devices: 212 us -> 184 us
  local copies, waits for them, and re-layouts: 41.8 us -> 35.9 us
    psum x1 -> x2, waiting for transfers between devices: 133 us -> 105 us  [the longest x1 68.6 us: on_device(): lax.psum(lax.psum(map_terms, axis_name='dp'), axis_name='seq')]
    unnamed x75 -> x69, local copies, waits for them, and re-layouts: 18 us -> 15.8 us
  transfers between devices with their start and end apart: 7 -> 8, of which waited for: 4 -> 5; matrix products, arithmetic and copies ran while one was open for 26% -> 29% of each run, Pallas kernels for 0% -> 0%
where the time goes in v1:
time: 345 us; the launch traced here: 343 us
  waiting for transfers between devices  184 us (53%)
  matrix products  78.7 us (23%)
  local copies, waits for them, and re-layouts  35.9 us (10%)
  other arithmetic  22.5 us (7%)
  between operations  14.4 us (4%)
  starting transfers between devices  7.3 us (2%)
    all_gather x2, waiting for transfers between devices, entering(): gathered = lax.all_gather(shard.astype(jnp.bfloat16), axis)  69 us
    psum x1, waiting for transfers between devices, on_device(): lax.psum(lax.psum(map_terms, axis_name='dp'), axis_name='seq')  68.6 us
    dot_general x16, matrix products, plain(): return jnp.einsum(form, left, right, preferred_element_type=jnp.float32)  58.8 us
    psum x1, waiting for transfers between devices, on_device(): lax.psum(map_terms, axis_name='dp')  36.7 us
    dot_general x8, matrix products, exact(): jnp.einsum(form, left.astype(jnp.float32), right.astype(jnp.float32), pre...  19.9 us
    unnamed x69, local copies, waits for them, and re-layouts  15.8 us
    ppermute x4, waiting for transfers between devices, passed_along(): return lax.ppermute(block, axis, route)  10 us
    add x7, other arithmetic, add_up(): return earlier + later  8.98 us
  transfers between devices with their start and end apart: 8, of which 5 were waited for; matrix products, arithmetic and copies ran while one was open for 29% of the time, Pallas kernels for 0%

profile of v1, /device:TPU:0, one launch (start us, length us, event | category | flops | bytes accessed | tf_op | source)
XLA Modules:
  0.0 343.5 jit_solution(16534069222115704418)
XLA Ops:
  8.4 1.3 copy.140
  10.4 2.8 multiply_reduce_fusion
  13.3 3.2 reverse.4
  17.7 1.4 fusion.57
  19.1 1.4 fusion.34
  20.5 69.0 %all-gather.7.cloned.1.call-done = bf16[128,128,128]{2,1,0:T(8,128)(2,1)} async-done(((bf16[16,128,128]{2,1,0:T(8,128)(2,1)}), bf16[128,128,128]{2,1,0:T(8,128)(2,1)}) %all-gather.7.cloned.1.call-update) | async-done | bytes 4194320 | tf_op jit(solution)/shard_map/all_gather | solution.py:15
  89.6 9.2 %while.23 = (s32[]{:T(128)}, f32[16,128,128]{2,1,0:T(8,128)S(1)}, s32[]{:T(128)}, bf16[8,16,128,128]{3,2,1,0:T(8,128)(2,1)}, s32[]{:T(128)}, /*index=5*/s32[]{:T(128)}, s32[]{:T(128)}, s32[]{:T(128)}) while((s32[]{:T(128)}, f32[16,128,128]{2,1,0:T(8,128)S(1)}, s32[]{:T(128)}, bf16[8,16,128,128]{3,2,1,0:T(8,128)(2,1)}, s32[]{:T(128)}, ...), condition=%wide.region_8.9_spmd, body=%wide.region_7.8_spmd.sunk | while | flops 524294 | bytes 2621575 | solution.py:22
  89.6 1.3 convert_add_fusion.5
  90.9 1.3 convert_add_fusion.5
  92.2 1.3 convert_add_fusion.5
  93.5 1.3 convert_add_fusion.5
  94.8 1.3 convert_add_fusion.5
  98.8 2.0 select_add_fusion
  100.8 2.3 fusion.14
  105.5 2.8 fusion.112
  109.5 2.0 collective-permute-start
  112.2 2.2 collective-permute-start.1
  115.9 5.2 %collective-permute-done = bf16[16,64,128]{2,1,0:T(8,128)(2,1)} collective-permute-done((bf16[16,64,128]{2,1,0:T(8,128)(2,1)}, bf16[16,64,128]{2,1,0:T(8,128)(2,1)}, u32[]{:S(2)}, u32[]{:S(2)}) %collective-permute-start) | collective-permute-done | bytes 262176 | tf_op jit(solution)/shard_map/ppermute | solution.py:28
  122.1 4.9 %collective-permute-done.1 = bf16[16,64,128]{2,1,0:T(8,128)(2,1)} collective-permute-done((bf16[16,64,128]{2,1,0:T(8,128)(2,1)}, bf16[16,64,128]{2,1,0:T(8,128)(2,1)}, u32[]{:S(2)}, u32[]{:S(2)}) %collective-permute-start.1) | collective-permute-done | bytes 262176 | tf_op jit(solution)/shard_map/ppermute | solution.py:28
  128.0 1.8 convolution_bitcast_fusion
  131.6 1.3 fusion.113
  132.9 15.4 %fusion.51 = f32[16,2,128,128]{3,2,1,0:T(8,128)} fusion(bf16[16,2,64,128]{3,2,1,0:T(8,128)(2,1)} %bitcast.171, f32[16,2,64,128]{3,2,1,0:T(8,128)} %convolution_bitcast_fusion, f32[16,2,64,128]{3,2,1,0:T(8,128)} %get-tuple-element.151, f32[16,2,64]{2,1,0:T(2,128)S(1)} %get-tuple-element.150), kind=kOutput, calls=%fused_computation.71 | convolution fusion | flops 68946048 | bytes 4726784 | tf_op jit(solution)/shard_map/hncs,hncd->hnsd/dot_general | solution.py:32
  148.3 1.8 fusion.81
  150.1 1.5 collective-permute-start.2
  151.6 7.1 %fusion.83 = f32[16,2,128,128]{3,2,1,0:T(8,128)} fusion(bf16[16,2,64,128]{3,2,1,0:T(8,128)(2,1)S(1)} %bitcast.154, f32[16,2,64]{2,1,0:T(2,128)S(1)} %get-tuple-element.150, f32[16,2,64,128]{3,2,1,0:T(8,128)} %copy-done.19, pred[2,64,128]{2,1,0:T(8,128)(4,1)S(1)} %fusion.86), kind=kOutput, calls=%fused_computation.111 | convolution fusion | flops 68421760 | bytes 3694592 | tf_op jit(solution)/shard_map/hncs,hncd->hnsd/dot_general | solution.py:32
  158.7 1.8 fusion.82
  160.5 14.2 %convolution_convert_fusion.2 = bf16[16,2,64,128]{3,2,1,0:T(8,128)(2,1)} fusion(f32[16,2,64,128]{3,2,1,0:T(8,128)} %convolution_bitcast_fusion, bf16[16,2,64,128]{3,2,1,0:T(8,128)(2,1)S(1)} %bitcast.161, bf16[16,2,64,128]{3,2,1,0:T(8,128)(2,1)} %bitcast.173, f32[16,2,64,128]{3,2,1,0:T(8,128)} %get-tuple-element.151, f32[16,2,64]{2,1,0:T(2,128)S(1)} %get-tuple-element.150), kind=kOutput, calls=%fused_computation.43 | convolution fusion | flops 71305344 | bytes 3678208 | tf_op jit(solution)/shard_map/hncs,hnsd->hncd/dot_general | solution.py:32
  174.6 1.9 slice.58
  177.8 1.4 copy.114
  182.3 1.4 fusion.49
  184.8 2.0 copy.127
  187.7 1.8 fusion.114
  190.6 1.4 convolution_select_fusion.1
  192.0 1.6 fusion.115
  193.6 2.1 fusion.4
  195.9 5.7 %fusion.17 = f32[16,2,64,128]{3,2,1,0:T(8,128)S(1)} fusion(f32[16,2,64,128]{3,2,1,0:T(8,128)} %fusion.115, bf16[16,2,64,128]{3,2,1,0:T(8,128)(2,1)S(1)} %bitcast.155, f32[1,16,128,128]{3,2,1,0:T(8,128)} %slice.49, f32[16,128,128]{2,1,0:T(8,128)S(1)} %get-tuple-element.86), kind=kOutput, calls=%fused_computation.20 | convolution fusion | flops 403963904 | bytes 4718592 | tf_op jit(solution)/shard_map/hncd,nhfd->hncf/dot_general | solution.py:36
  203.1 1.3 fusion.31
  204.8 4.0 %fusion.48 = bf16[16,2,64,128]{3,2,1,0:T(8,128)(2,1)S(1)} fusion(f32[16,2,128,128]{3,2,1,0:T(8,128)} %fusion.83, f32[16,1,64,128]{3,2,1,0:T(8,128)} %bitcast_convert_fusion, f32[16,1,64,128]{3,2,1,0:T(8,128)} %slice.58, f32[16,2,64,128]{3,2,1,0:T(8,128)} %fusion.4, f32[16,2,64,64]{3,2,1,0:T(8,128)} %convolution_select_fusion.1, ...), kind=kOutput, calls=%fused_computation.62 | convolution fusion | flops 203161600 | bytes 4718592 | tf_op jit(solution)/shard_map/hncs,hncd->hnsd/dot_general | solution.py:36
  209.9 2.1 broadcast_in_dim_reshape.23
  213.3 2.1 copy.126
  215.4 36.7 %all-reduce.4.cloned.1.call-done = f32[16,128,128]{1,2,0:T(8,128)} async-done(((f32[16,128,128]{1,2,0:T(8,128)}), f32[16,128,128]{1,2,0:T(8,128)}) %all-reduce.4.cloned.1.call-update) | async-done | bytes 1048592 | tf_op jit(solution)/shard_map/psum | solution.py:205
  252.1 1.3 convolution_convert_fusion.1
  253.4 2.0 copy.125
  255.5 2.5 fusion.10
  259.0 5.3 %fusion.35 = bf16[16,2,64,128]{3,2,1,0:T(8,128)(2,1)S(1)} fusion(f32[16,2,64,128]{3,2,1,0:T(8,128)S(1)} %fusion.33, bf16[16,2,64,128]{3,2,1,0:T(8,128)(2,1)S(1)} %bitcast.143, bf16[16,2,64,128]{3,2,1,0:T(8,128)(2,1)S(1)} %bitcast.169, f32[16,2,64]{2,1,0:T(2,128)S(1)} %get-tuple-element.150, f32[16,2,64,128]{3,2,1,0:T(8,128)} %copy-done.19, ...), kind=kOutput, calls=%fused_computation.40 | convolution fusion | flops 71043200 | bytes 3694592 | tf_op jit(solution)/shard_map/hncs,hnsd->hncd/dot_general | solution.py:32
  265.7 68.6 %all-reduce.6.cloned.1.call-done = f32[16,128,128]{1,2,0:T(8,128)} async-done(((f32[16,128,128]{1,2,0:T(8,128)}), f32[16,128,128]{1,2,0:T(8,128)}) %all-reduce.6.cloned.1.call-update) | async-done | bytes 1048592 | tf_op jit(solution)/shard_map/psum | solution.py:205
  334.3 1.3 broadcast_multiply_fusion
  335.6 1.3 copy.128
  (111 shorter events, 29.4 us)
Async XLA Ops:
  7.2 2.6 copy-start
  7.2 82.3 %all-gather.7.cloned.1.call-start = ((), (), s32[]{:S(2)}) async-start(), calls=%async_computation.3 | async-start | bytes 4718592 | tf_op jit(solution)/shard_map/all_gather | solution.py:15
  8.4 1.7 copy-start.14
  10.1 3.1 copy-start.6
  13.2 182.5 %all-gather.5.cloned.1.call-start = ((), (), s32[]{:S(2)}) async-start(), calls=%async_computation.2 | async-start | bytes 4718592 | tf_op jit(solution)/shard_map/all_gather | solution.py:15
  13.3 3.2 copy-start.25
  16.5 1.1 copy-start.26
  16.6 0.8 copy-start.10
  17.7 2.8 copy-start.16
  89.6 9.2 %copy-start.28 = (pred[2]{0:T(512)(128)(4,1)S(1)}, pred[2]{0:T(512)(128)(4,1)}, u32[]{:S(2)}) copy-start(pred[2]{0:T(512)(128)(4,1)} %constant.73.clone.1) | copy-start | bytes 10
  100.8 3.4 copy-start.1
  100.8 2.3 copy-start.4
  103.1 1.2 copy-start.18
  104.2 1.4 copy-start.11
  105.5 2.8 copy-start.27
  108.3 143.8 %all-reduce.4.cloned.1.call-start = ((), (), s32[]{:S(2)}) async-start(), calls=%async_computation | async-start | bytes 2097152 | tf_op jit(solution)/shard_map/psum | solution.py:205
  109.5 11.6 %collective-permute-start = (bf16[16,64,128]{2,1,0:T(8,128)(2,1)}, bf16[16,64,128]{2,1,0:T(8,128)(2,1)}, u32[]{:S(2)}, u32[]{:S(2)}) collective-permute-start(bf16[16,64,128]{2,1,0:T(8,128)(2,1)} %get-tuple-element.134), channel_id=1, source_target_pairs={{0,4},{4,8},{8,12},{12,16},{16,20},{20,24},{24,28},{1,5},{5,9},{9,... | collective-permute-start | bytes 786440 | tf_op jit(solution)/shard_map/ppermute | solution.py:28
  112.2 14.7 %collective-permute-start.1 = (bf16[16,64,128]{2,1,0:T(8,128)(2,1)}, bf16[16,64,128]{2,1,0:T(8,128)(2,1)}, u32[]{:S(2)}, u32[]{:S(2)}) collective-permute-start(bf16[16,64,128]{2,1,0:T(8,128)(2,1)} %get-tuple-element.138), channel_id=1, source_target_pairs={{0,4},{4,8},{8,12},{12,16},{16,20},{20,24},{24,28},{1,5},{5,9},{9,... | collective-permute-start | bytes 786440 | tf_op jit(solution)/shard_map/ppermute | solution.py:28
  114.4 6.7 %copy-start.24 = (bf16[16,64,128]{2,1,0:T(8,128)(2,1)S(1)}, bf16[16,64,128]{2,1,0:T(8,128)(2,1)}, u32[]{:S(2)}) copy-start(bf16[16,64,128]{2,1,0:T(8,128)(2,1)} %get-tuple-element.135) | copy-start | bytes 786436
  115.8 14.0 %copy-start.22 = (bf16[16,128,128]{2,1,0:T(8,128)(2,1)}, bf16[16,128,128]{2,1,0:T(8,128)(2,1)S(1)}, u32[]{:S(2)}) copy-start(bf16[16,128,128]{2,1,0:T(8,128)(2,1)S(1)} %copy.106) | copy-start | bytes 1572868
  122.1 8.5 %copy-start.23 = (bf16[16,128,128]{2,1,0:T(8,128)(2,1)}, bf16[16,128,128]{2,1,0:T(8,128)(2,1)S(1)}, u32[]{:S(2)}) copy-start(bf16[16,128,128]{2,1,0:T(8,128)(2,1)S(1)} %pad_maximum_fusion.6) | copy-start | bytes 1572868
  127.9 1.8 copy-start.20
  130.6 1.0 copy-start.19
  150.1 31.2 %collective-permute-start.2 = (bf16[16,64,128]{2,1,0:T(8,128)(2,1)}, bf16[16,64,128]{2,1,0:T(8,128)(2,1)}, u32[]{:S(2)}, u32[]{:S(2)}) collective-permute-start(bf16[16,64,128]{2,1,0:T(8,128)(2,1)} %fusion.81), channel_id=1, source_target_pairs={{4,0},{8,4},{12,8},{16,12},{20,16},{24,20},{28,24},{5,1},{9,5},{13... | collective-permute-start | bytes 786440 | tf_op jit(solution)/shard_map/ppermute | solution.py:28
  176.5 10.3 %collective-permute-start.3 = (bf16[16,64,128]{2,1,0:T(8,128)(2,1)}, bf16[16,64,128]{2,1,0:T(8,128)(2,1)S(1)}, u32[]{:S(2)}, u32[]{:S(2)}) collective-permute-start(bf16[16,64,128]{2,1,0:T(8,128)(2,1)} %fusion.82), channel_id=1, source_target_pairs={{4,0},{8,4},{12,8},{16,12},{20,16},{24,20},{28,24},{5,1},{9,5},{13... | collective-permute-start | bytes 786440 | tf_op jit(solution)/shard_map/ppermute | solution.py:28
  189.5 2.5 copy-start.5
  190.6 3.0 copy-start.2
  195.8 5.7 %copy-start.7 = (f32[16,128,128]{2,1,0:T(8,128)S(1)}, f32[16,128,128]{2,1,0:T(8,128)}, u32[]{:S(2)}) copy-start(f32[16,128,128]{2,1,0:T(8,128)} %copy-done.6) | copy-start | bytes 3145732
  201.6 1.1 copy-start.15
  201.6 1.5 copy-start.8
  201.6 1.5 copy-start.17
  201.9 0.8 copy-start.12
  204.5 129.8 %all-reduce.6.cloned.1.call-start = ((), (), s32[]{:S(2)}) async-start(), calls=%async_computation.1 | async-start | bytes 2097152 | tf_op jit(solution)/shard_map/psum | solution.py:205
  208.8 3.2 copy-start.9
  213.3 38.9 %copy-start.13 = (bf16[16,128,128]{2,1,0:T(8,128)(2,1)S(1)}, bf16[16,128,128]{2,1,0:T(8,128)(2,1)}, u32[]{:S(2)}) copy-start(bf16[16,128,128]{2,1,0:T(8,128)(2,1)} %copy-done.12) | copy-start | bytes 1572868
  255.5 2.5 copy-start.3
  258.0 1.0 copy-start.21
Sparse Core Ops, SparseCore 0:
  13.3 76.0 all-gather.6
  108.4 81.4 all-gather.4
  204.6 47.4 all-reduce.3
  255.9 78.3 all-reduce.5
